TPU v7x, 256 devices: a whole 4x4x8 slice. The times are simulated.
256 devices in a mesh: dom: 4 (over y), pencil: 64 (over x, z, core).
Axes of the slice: x: 4, y: 4, z: 8, core: 2. Of those that a mesh axis runs over, the one named last changes fastest.
Arguments:
- modes_now: float32 [4, 256, 256, 256], P('dom', 'pencil'), may hold values from -6 to 6
- modes_prev: float32 [4, 256, 256, 256], P('dom', 'pencil'), may hold values from -6 to 6
- extents: int32 [4, 2], replicated, may hold values from 128 to 256, as said below
- strips: int32 [8, 6], replicated, may hold values from 0 to 256, as said below
Outputs:
- modes_next: float32 [4, 256, 256, 256], P('dom', 'pencil')
- modes_last: float32 [4, 256, 256, 256], P('dom', 'pencil')
- pressure: float32 [4, 256, 256, 256], P('dom', None, 'pencil')
Inputs may be any that keep to these rules, and one draw needn't show every extreme that they name: `extents`: row p holds partition p's lengths in cells along the first and the third dimension of its box; along the second dimension every partition has 256 cells. One partition has 256 along both, and two have 256 along the first. `strips`: row s is one strip (p, q, f, a, b, e): owner partition p, touching partition q with q != p, face f (0: p's face at third index 0 meets q's face at its last third index; 1: p's last face meets q's face at third index 0), start a in p and start b in q along the first dimension, extent e >= 1 with a + e at most p's first length and b + e at most q's. A strip covers all 256 cells of the second dimension. Some strip has e = 256.
All inputs are finite; a program needn't handle non-finite values.
Results may differ from a plain program's by a relative error of at most 0.0001.
Values sent between devices are 32-bit elements; how exact they have to be, the bound alone decides.
A program may use at most 64 MiB of HBM per device.

v0:
```python
import functools
import math

import jax
import jax.numpy as jnp
from jax import lax
from jax.experimental import pallas as pl
from jax.experimental.pallas import tpu as pltpu
from jax.sharding import PartitionSpec as P

MESH = pl.DeviceIdType.MESH
F32, BF16, I32 = jnp.float32, jnp.bfloat16, jnp.int32
DOMS, PENCILS, BOX, ROWS = 4, 64, 256, 4
EVERYONE = DOMS * PENCILS
STRIPS = 8
HALF_PI = math.pi / 2.0
COUPLING = (1.5, -0.15, 2.0 / 180.0)
GAIN = (
    0.9999999999869928, -0.08333333316111119, 0.0027777774047159443, -4.960287119518586e-05,
    5.510286659542367e-07, -4.151822786228911e-09, 2.058914415718572e-11,
)
SINE = (
    1.5707963267681446, -0.6459640955780578, 0.07969260371703452, -0.004681657795344663,
    0.00016025469086571314, -3.431829236433259e-06,
)


def poly(coefs, t):
    value = jnp.full_like(t, coefs[-1])
    for coef in coefs[-2::-1]:
        value = value * t + coef
    return value


def split(value):
    high = value.astype(BF16)
    return high, (value - high.astype(F32)).astype(BF16)


def dot(left, right, left_dim, right_dim):
    return lax.dot_general(left, right, (((left_dim,), (right_dim,)), ((), ())), preferred_element_type=F32)


def dot3(left, right, left_dim=1, right_dim=0):
    return (
        dot(left[0], right[0], left_dim, right_dim)
        + dot(left[0], right[1], left_dim, right_dim)
        + dot(left[1], right[0], left_dim, right_dim)
    )


def dot_thin(value, right, right_dim):
    rows = value.shape[0]
    high = value.astype(BF16).astype(F32)
    left = jnp.concatenate([high, value - high], axis=0).astype(BF16)
    total = dot(left, right[0], 1, right_dim) + dot(left, right[1], 1, right_dim)
    return total[:rows] + total[rows:]


def iota(shape, dim):
    return lax.broadcasted_iota(I32, shape, dim)


def row_of(scalar):
    return jnp.full((1, BOX), scalar.astype(F32))


def cosines(length, waves, cells):
    width = max(waves.shape[1], cells.shape[1])
    long = jnp.full((1, width), length.astype(F32))
    inverse = 1.0 / long
    n = (waves * (2 * cells + 1)).astype(F32)
    turns = jnp.floor(n * (0.25 * inverse) + 0.5)
    u = 1.0 - jnp.abs(n - turns * (4.0 * long)) * inverse
    scale = jnp.where(waves == 0, jnp.sqrt(inverse), jnp.sqrt(2.0 * inverse))
    value = scale * u * poly(SINE, u * u)
    return jnp.where((waves < length) & (cells < length), value, 0.0)


def slot_cells(length_z, slots):
    return jnp.where(slots < 3, slots, length_z - 1 - (slots - 3))


def coupled_kernel(
    ext, strips, now, prev,
    one_out, two_out, pieces, xt_hi, xt_lo,
    m0, m_old, pushed, twice, free, sent, got, back, returned,
    tx_hi, tx_lo, response, edge_hi, edge_lo, tz_hi, tz_lo, ty_hi, ty_lo, mid_hi, mid_lo, turn,
    load_sem, own_sem, send_sem, recv_sem,
):
    dom, pencil = lax.axis_index("dom"), lax.axis_index("pencil")
    me = dom * PENCILS + pencil
    load_now = pltpu.make_async_copy(now, m0, load_sem.at[0])
    load_prev = pltpu.make_async_copy(prev, m_old, load_sem.at[1])
    load_now.start()
    load_prev.start()
    barrier = pltpu.get_barrier_semaphore()

    def device_of(step):
        peer = lax.rem(me + step, EVERYONE)
        return peer, (lax.div(peer, PENCILS), lax.rem(peer, PENCILS))

    def greet(first, count):
        for j in range(count):
            pl.semaphore_signal(barrier, inc=1, device_id=device_of(first + j)[1], device_id_type=MESH)

    def send_rows(source, target, leg, first, count):
        for j in range(count):
            peer, device = device_of(first + j)
            pltpu.make_async_remote_copy(
                src_ref=source.at[pl.ds(peer, 1)],
                dst_ref=target.at[pl.ds(me, 1)],
                send_sem=send_sem.at[leg],
                recv_sem=recv_sem.at[leg],
                device_id=device,
                device_id_type=MESH,
            ).start()

    def wait_rows(source, target, leg):
        pltpu.make_async_copy(source.at[pl.ds(me, 1)], target.at[pl.ds(me, 1)], own_sem.at[leg]).wait()
        pltpu.make_async_remote_copy(
            src_ref=source.at[pl.ds(0, EVERYONE - 1)],
            dst_ref=target.at[pl.ds(0, EVERYONE - 1)],
            send_sem=send_sem.at[leg],
            recv_sem=recv_sem.at[leg],
            device_id=device_of(1)[1],
            device_id_type=MESH,
        ).wait()

    length_x, length_z = ext[dom, 0], ext[dom, 1]

    lanes = iota((BOX, 128), 1)
    slots = lax.rem(lanes, 8)
    table = cosines(length_z, iota((BOX, 128), 0), slot_cells(length_z, slots))
    face_hi, face_lo = split(jnp.where(slots < 6, table, 0.0))
    waves_z = iota((1, BOX), 1)
    along_z = waves_z.astype(F32) * HALF_PI / row_of(length_z)
    along_z = along_z * along_z
    live_z = (waves_z < length_z).astype(F32)
    greet(1, 7)
    load_now.wait()
    load_prev.wait()
    block = 32
    groups = lax.div(iota((block, 128), 1), 8)

    def gather_faces(step, carry):
        at = pl.ds(pl.multiple_of(step * block, block), block)
        along_y = (iota((block, BOX), 0) + step * block).astype(F32) * (HALF_PI / BOX)
        along_y = along_y * along_y
        message = jnp.zeros((block, 128), F32)
        for a in range(ROWS):
            wave = pencil * ROWS + a
            along_x = row_of(wave) * HALF_PI / row_of(length_x)
            live = live_z * (jnp.full((1, BOX), wave) < length_x).astype(F32)
            t = along_y + (along_z + along_x * along_x)
            gain = poly(GAIN, t)
            twice_cos = 2.0 - t * gain
            here = m0[a, at, :]
            ahead = live * (twice_cos * here - m_old[a, at, :])
            pushed[a, at, :] = live * gain
            twice[a, at, :] = twice_cos
            free[a, at, :] = ahead
            for u, value in enumerate((here, ahead)):
                faces = dot3(split(value), (face_hi, face_lo))
                message = jnp.where(groups == u * ROWS + a, faces, message)
        sent[at, :] = message
        greet(8 + step * 31, 31)
        return carry

    lax.fori_loop(0, BOX // block, gather_faces, 0)
    pl.semaphore_wait(barrier, EVERYONE - 1)
    pltpu.make_async_copy(sent.at[pl.ds(me, 1)], got.at[pl.ds(me, 1)], own_sem.at[0]).start()
    send_rows(sent, got, 0, 1, 7)

    def x_tables(step, carry):
        send_rows(sent, got, 0, 8 + step * 10, 10)
        part, a = lax.div(step, ROWS), lax.rem(step, ROWS)
        at = pl.ds(pl.multiple_of(a * PENCILS, PENCILS), PENCILS)
        high, low = split(
            cosines(ext[part, 0], iota((PENCILS, BOX), 0) * ROWS + a, iota((PENCILS, BOX), 1))
        )
        tx_hi[part, at, :] = high
        tx_lo[part, at, :] = low
        return carry

    lax.fori_loop(0, DOMS * ROWS, x_tables, 0)

    def responses(step, carry):
        send_rows(sent, got, 0, 168 + step * 11, 11)
        part, half = lax.div(step, 2), lax.rem(step, 2)
        long_x, long_z = ext[part, 0], ext[part, 1]
        slot = iota((8, BOX), 0)
        rows = jnp.where(slot < 6, cosines(long_z, iota((8, BOX), 1), slot_cells(long_z, slot)), 0.0)
        pairs = jnp.concatenate([rows * rows[i : i + 1] for i in range(8)], axis=0)
        order = iota((128, BOX), 0) + half * 128
        waves = lax.rem(order, PENCILS) * ROWS + lax.div(order, PENCILS)
        along_x = waves.astype(F32) * HALF_PI / row_of(long_x)
        across = waves_z.astype(F32) * HALF_PI / row_of(long_z)
        along_y = row_of(me) * (HALF_PI / BOX)
        gain = poly(GAIN, along_x * along_x + (across * across + along_y * along_y))
        gain = jnp.where((waves < long_x) & (iota((128, BOX), 1) < long_z), gain, 0.0)
        response[part, half] = dot3(split(pairs), split(gain), 1, 1)
        return carry

    lax.fori_loop(0, DOMS * 2, responses, 0)

    def of_strip(strip_index, field):
        value = jnp.zeros_like(strip_index)
        for e in range(STRIPS):
            value = jnp.where(strip_index == e, strips[e, field], value)
        return value

    wide = iota((8 * STRIPS, 32), 0)
    index, depth = lax.div(wide, 8), lax.rem(wide, 8)
    column = iota((8 * STRIPS, 32), 1)
    part, slot = lax.div(column, 8), lax.rem(column, 8)
    face = of_strip(index, 2)

    def weights(parts, side):
        other = slot - 3 * side
        reach = depth + other
        value = jnp.where(reach == 0, 0.25 * COUPLING[0], jnp.where(reach == 1, 0.25 * COUPLING[1], 0.25 * COUPLING[2]))
        hit = (parts == part) & (other >= 0) & (other < 3) & (depth < 3) & (reach < 3)
        return jnp.where(hit, value, 0.0)

    takes = split(jnp.concatenate([weights(of_strip(index, 1), 1 - face), weights(of_strip(index, 0), face)], axis=0))
    tall = iota((32, 8 * STRIPS), 1)
    index, depth = lax.div(tall, 8), lax.rem(tall, 8)
    column = iota((32, 8 * STRIPS), 0)
    part, slot = lax.div(column, 8), lax.rem(column, 8)
    gives = (part == of_strip(index, 0)) & (slot == 3 * of_strip(index, 2) + depth) & (depth < 3)
    gives = jnp.where(gives, 1.0, 0.0).astype(BF16)
    index = lax.div(iota((8 * STRIPS, BOX), 0), 8)
    cells = iota((8 * STRIPS, BOX), 1)
    start = of_strip(index, 3)
    inside = (cells >= start) & (cells < start + of_strip(index, 5))

    def force(face_modes):
        faces = jnp.concatenate(
            [dot_thin(face_modes[p], (tx_hi[p], tx_lo[p]), 0) for p in range(DOMS)], axis=0
        )
        taken = dot3(takes, split(faces))
        shifted = [
            pltpu.roll(taken[8 * e : 8 * e + 8], lax.rem(strips[e, 3] - strips[e, 4] + BOX, BOX), 1)
            for e in range(STRIPS)
        ]
        gap = split(jnp.where(inside, jnp.concatenate(shifted, axis=0) - taken[8 * STRIPS :], 0.0))
        forcing = dot(gives, gap[0], 1, 0) + dot(gives, gap[1], 1, 0)
        return [dot_thin(forcing[8 * p : 8 * p + 8], (tx_hi[p], tx_lo[p]), 1) for p in range(DOMS)]

    wait_rows(sent, got, 0)
    first, second = [], []
    for pair in range(2):
        turned = got[128 * pair : 128 * pair + 128, :].T
        for p in range(2):
            for u, held in enumerate((first, second)):
                held.append(
                    jnp.concatenate(
                        [
                            turned[8 * (u * ROWS + a) : 8 * (u * ROWS + a) + 8, PENCILS * p : PENCILS * (p + 1)]
                            for a in range(ROWS)
                        ],
                        axis=1,
                    )
                )
    force_one = force(first)
    answered = []
    for p in range(DOMS):
        both = jnp.concatenate([response[p, 0], response[p, 1]], axis=1).reshape(8, 8, BOX)
        answered.append(second[p] + jnp.sum(both * force_one[p][None], axis=1))
    force_two = force(answered)
    for pair in range(2):
        rows = [
            jnp.concatenate(
                [forces[2 * pair + p][:, PENCILS * a : PENCILS * (a + 1)] for p in range(2)], axis=1
            )
            for forces in (force_one, force_two)
            for a in range(ROWS)
        ]
        rows.append(jnp.zeros((64, 128), F32))
        back[128 * pair : 128 * pair + 128, :] = jnp.concatenate(rows, axis=0).T
    pltpu.make_async_copy(back.at[pl.ds(me, 1)], returned.at[pl.ds(me, 1)], own_sem.at[1]).start()
    send_rows(back, returned, 1, 1, 15)

    def late_tables(step, carry):
        send_rows(back, returned, 1, 16 + step * 30, 30)
        at = pl.ds(pl.multiple_of(step * 32, 32), 32)
        near, far = iota((32, BOX), 0) + step * 32, iota((32, BOX), 1)
        tz_hi[at, :], tz_lo[at, :] = split(cosines(length_z, near, far))
        ty_hi[at, :], ty_lo[at, :] = split(cosines(jnp.int32(BOX), far, near))
        rows = iota((128, BOX), 0)
        cells = lax.rem(rows, 8)
        values = cosines(length_z, iota((128, BOX), 1), slot_cells(length_z, cells))
        values = jnp.where((cells < 6) & (lax.div(rows, 8) == step), values, 0.0)
        edge_hi[step], edge_lo[step] = split(values)
        return carry

    lax.fori_loop(0, 8, late_tables, 0)
    wait_rows(back, returned, 1)
    come = split(returned[...])
    top = iota((32, 8, BOX), 1) < 4
    own_turns = []
    for pair in range(2):
        planes = []
        for a in (2 * pair, 2 * pair + 1):
            wave = pencil * ROWS + a
            live = live_z * (jnp.full((1, BOX), wave) < length_x).astype(F32)
            for half in range(2):
                at = slice(128 * half, 128 * half + 128)
                left = (come[0][at], come[1][at])
                gain = pushed[a, at, :]
                m1 = free[a, at, :] + gain * dot3(left, (edge_hi[a], edge_lo[a]))
                one_out[a, at, :] = m1
                m2 = live * (twice[a, at, :] * m1 - m0[a, at, :]) + gain * dot3(
                    left, (edge_hi[ROWS + a], edge_lo[ROWS + a])
                )
                two_out[a, at, :] = m2
                middle = dot3(split(m2), (tz_hi[...], tz_lo[...]))
                mid_hi[at, :], mid_lo[at, :] = split(middle)
            plane = dot3((ty_hi[...], ty_lo[...]), (mid_hi[...], mid_lo[...]))
            planes.append(plane.reshape(32, 8, BOX))
        even = jnp.where(top, planes[0], pltpu.roll(planes[1], 4, 1))
        odd = jnp.where(top, pltpu.roll(planes[0], 4, 1), planes[1])
        for side in range(2):
            turn[side, pair, :, 0] = even[:, :, 128 * side : 128 * side + 128]
            turn[side, pair, :, 1] = odd[:, :, 128 * side : 128 * side + 128]
        own = pltpu.make_async_copy(
            turn.at[:, pair, lax.div(pencil, 2), lax.rem(pencil, 2)], pieces.at[:, pair, pencil], own_sem.at[2 + pair]
        )
        own.start()
        own_turns.append(own)

        def send_turn(step, carry):
            peer = lax.rem(pencil + step, PENCILS)
            pltpu.make_async_remote_copy(
                src_ref=turn.at[:, pair, lax.div(peer, 2), lax.rem(peer, 2)],
                dst_ref=pieces.at[:, pair, pencil],
                send_sem=send_sem.at[2 + pair],
                recv_sem=recv_sem.at[2 + pair],
                device_id=(dom, peer),
                device_id_type=MESH,
            ).start()
            return carry

        lax.fori_loop(1, PENCILS, send_turn, 0)

    def turned_tables(step, carry):
        at = pl.ds(pl.multiple_of(step * 32, 32), 32)
        order = iota((32, BOX), 1)
        waves = lax.rem(lax.div(order, 2), PENCILS) * ROWS + lax.div(order, 128) * 2 + lax.rem(order, 2)
        xt_hi[at, :], xt_lo[at, :] = split(cosines(length_x, waves, iota((32, BOX), 0) + step * 32))
        return carry

    lax.fori_loop(0, 8, turned_tables, 0)
    for pair in range(2):
        own_turns[pair].wait()
        pltpu.make_async_remote_copy(
            src_ref=pieces.at[:, pair, pl.ds(0, PENCILS - 1)],
            dst_ref=pieces.at[:, pair, pl.ds(0, PENCILS - 1)],
            send_sem=send_sem.at[2 + pair],
            recv_sem=recv_sem.at[2 + pair],
            device_id=(dom, lax.rem(pencil + 1, PENCILS)),
            device_id_type=MESH,
        ).wait()


def spread_kernel(pieces, xt_hi, xt_lo, one, two, one_out, two_out, pressure, sems):
    copies = [
        pltpu.make_async_copy(one, one_out, sems.at[0]),
        pltpu.make_async_copy(two, two_out, sems.at[1]),
    ]
    for copy in copies:
        copy.start()
    table = (xt_hi[...], xt_lo[...])
    for y in range(ROWS):
        for side in range(2):
            piece = pieces[pl.ds(side * BOX * ROWS + y, BOX, stride=ROWS), :]
            pressure[:, y, 128 * side : 128 * side + 128] = dot3(table, split(piece))
    for copy in copies:
        copy.wait()


def on_device(modes_now, modes_prev, extents, strips):
    vmem, smem, anywhere = (
        pl.BlockSpec(memory_space=space) for space in (pltpu.VMEM, pltpu.SMEM, pl.ANY)
    )
    field = jax.ShapeDtypeStruct((ROWS, BOX, BOX), F32)
    half_table = jax.ShapeDtypeStruct((BOX, BOX), BF16)
    one, two, pieces, xt_hi, xt_lo = pl.pallas_call(
        coupled_kernel,
        out_shape=(field, field, jax.ShapeDtypeStruct((2, 2, PENCILS, 8, 128), F32), half_table, half_table),
        in_specs=[smem, smem, anywhere, anywhere],
        out_specs=[vmem] * 5,
        scratch_shapes=[pltpu.VMEM((ROWS, BOX, BOX), F32)] * 5
        + [pltpu.VMEM((EVERYONE, 128), F32)] * 4
        + [pltpu.VMEM((DOMS, BOX, BOX), BF16)] * 2
        + [pltpu.VMEM((DOMS, 2, 64, 128), F32)]
        + [pltpu.VMEM((2 * ROWS, 128, BOX), BF16)] * 2
        + [pltpu.VMEM((BOX, BOX), BF16)] * 6
        + [pltpu.VMEM((2, 2, PENCILS // 2, 2, 8, 128), F32)]
        + [pltpu.SemaphoreType.DMA((2,))]
        + [pltpu.SemaphoreType.DMA((4,))] * 3,
        compiler_params=pltpu.CompilerParams(has_side_effects=True, collective_id=1, vmem_limit_bytes=44 << 20),
        name="coupled",
    )(extents, strips, modes_now[0], modes_prev[0])
    one, two, pressure = pl.pallas_call(
        spread_kernel,
        out_shape=(field, field, jax.ShapeDtypeStruct((BOX, ROWS, BOX), F32)),
        in_specs=[vmem] * 5,
        out_specs=[anywhere, anywhere, vmem],
        scratch_shapes=[pltpu.SemaphoreType.DMA((2,))],
        compiler_params=pltpu.CompilerParams(vmem_limit_bytes=24 << 20),
        name="spread",
    )(pieces.reshape(2 * BOX * ROWS, 128), xt_hi, xt_lo, one, two)
    return (two[None], one[None], pressure[None])


def solution(mesh):
    return jax.shard_map(
        on_device,
        mesh=mesh,
        in_specs=(P("dom", "pencil", None, None), P("dom", "pencil", None, None), P(), P()),
        out_specs=(
            P("dom", "pencil", None, None),
            P("dom", "pencil", None, None),
            P("dom", None, "pencil", None),
        ),
        check_vma=False,
    )
```

profile of v0, /device:TPU:1, one launch (start us, length us, event | category | flops | bytes accessed | tf_op | source)
XLA Modules:
  0.0 70.8 jit_solution(15791631469976066485)
XLA Ops:
  0.6 0.0 copy-start.2
  0.6 0.8 %copy.7.ext = s32[4,2]{1,0:T(4,128)S(1)} copy(s32[4,2]{0,1:T(2,128)} %param.6) | data formatting | bytes 64 | tf_op args[2]
  1.4 0.0 copy-done.2
  1.4 0.0 copy-start
  1.4 1.2 %copy-done = f32[1,4,256,256]{3,2,1,0:T(8,128)S(1)} copy-done((f32[1,4,256,256]{3,2,1,0:T(8,128)S(1)}, f32[1,4,256,256]{3,2,1,0:T(8,128)}, u32[]{:S(2)}) %copy-start) | copy-done | bytes 1048600
  2.6 0.0 copy-start.1
  2.6 1.2 %copy-done.1 = f32[1,4,256,256]{3,2,1,0:T(8,128)S(1)} copy-done((f32[1,4,256,256]{3,2,1,0:T(8,128)S(1)}, f32[1,4,256,256]{3,2,1,0:T(8,128)}, u32[]{:S(2)}) %copy-start.1) | copy-done | bytes 1048600
  3.9 64.6 %coupled.1 = (f32[4,256,256]{2,1,0:T(8,128)S(1)}, f32[4,256,256]{2,1,0:T(8,128)S(1)}, f32[2,2,64,8,128]{4,3,2,1,0:T(8,128)S(1)}, bf16[256,256]{1,0:T(8,128)(2,1)S(1)}, bf16[256,256]{1,0:T(8,128)(2,1)S(1)}) custom-call(s32[4,2]{1,0:T(4,128)S(1)} %copy.7.ext, s32[8,6]{1,0:T(8,128)S(1)} %copy-done.2, f32[4,256,256]{2,1,0:T(8,128)S(1)} %bitcast.6, ...), custom_call_target="tpu_custom_call" | custom-call | tf_op jit(solution)/shard_map/coupled/pallas_call | solution.py:389
  68.5 2.4 %spread.1 = (f32[4,256,256]{2,1,0:T(8,128)}, f32[4,256,256]{2,1,0:T(8,128)}, f32[256,4,256]{2,1,0:T(4,128)}) custom-call(f32[2048,128]{1,0:T(8,128)S(1)} %bitcast.8, bf16[256,256]{1,0:T(8,128)(2,1)S(1)} %get-tuple-element.12.xt_hi, bf16[256,256]{1,0:T(8,128)(2,1)S(1)} %get-tuple-element.13.xt_lo, f32[4,256,256]{2,1,0:T(8,128)S(1)} %get-tuple-element.14.one, ...), custom_call_target="tpu_custom_call" | custom-call | tf_op jit(solution)/shard_map/spread/pallas_call | solution.py:406
Async XLA Ops:
  0.6 0.8 %copy-start.2 = (s32[8,6]{1,0:T(8,128)S(1)}, s32[8,6]{1,0:T(8,128)}, u32[]{:S(2)}) copy-start(s32[8,6]{1,0:T(8,128)} %strips.1) | copy-start | bytes 580
  1.4 1.2 %copy-start = (f32[1,4,256,256]{3,2,1,0:T(8,128)S(1)}, f32[1,4,256,256]{3,2,1,0:T(8,128)}, u32[]{:S(2)}) copy-start(f32[1,4,256,256]{3,2,1,0:T(8,128)} %param.4) | copy-start | bytes 3145732
  2.6 1.2 %copy-start.1 = (f32[1,4,256,256]{3,2,1,0:T(8,128)S(1)}, f32[1,4,256,256]{3,2,1,0:T(8,128)}, u32[]{:S(2)}) copy-start(f32[1,4,256,256]{3,2,1,0:T(8,128)} %param.5) | copy-start | bytes 3145732
where the time goes:
time: 71 us; the launch traced here: 70.8 us
  Pallas kernels  67 us (94%)
  local copies, waits for them, and re-layouts  3.22 us (5%)
    pallas_call x1, Pallas kernels, on_device(): pl.pallas_call(coupled_kernel, out_shape=(field, field, jax.ShapeDtypeStr...  64.6 us
    unnamed x7, local copies, waits for them, and re-layouts  3.22 us
    pallas_call x1, Pallas kernels, on_device(): pl.pallas_call(spread_kernel, out_shape=(field, field, jax.ShapeDtypeStru...  2.36 us

commit v1 on v0

--- a/solution.py
+++ b/solution.py
@@ -19,6 +19,12 @@
     0.9999999999869928, -0.08333333316111119, 0.0027777774047159443, -4.960287119518586e-05,
     5.510286659542367e-07, -4.151822786228911e-09, 2.058914415718572e-11,
 )
+PUSHED_GAIN = (
+    1.9999999838483329, -1.1666663858596251, 0.17222142001421806, -0.012598331258825314,
+    0.0005628010719150018, -1.6955597515164814e-05, 3.5301674212625207e-07, -4.241805096348839e-09,
+)
+MID = math.pi**2 / 8.0
+BULK = (1, 2, 16, 0)
 SINE = (
     1.5707963267681446, -0.6459640955780578, 0.07969260371703452, -0.004681657795344663,
     0.00016025469086571314, -3.431829236433259e-06,
@@ -82,39 +88,81 @@
 
 
 def coupled_kernel(
-    ext, strips, now, prev,
-    one_out, two_out, pieces, xt_hi, xt_lo,
+    ext_in, strips_in, now, prev,
+    one_out, two_out, pieces, late, xt_hi, xt_lo, zt_hi, zt_lo,
     m0, m_old, pushed, twice, free, sent, got, back, returned,
-    tx_hi, tx_lo, response, edge_hi, edge_lo, tz_hi, tz_lo, ty_hi, ty_lo, mid_hi, mid_lo, turn,
+    tx_hi, tx_lo, response, edge_hi, edge_lo, tz_hi, tz_lo, ty_hi, ty_lo, mid_hi, mid_lo, turn, lift, late_turn, ext, strips,
     load_sem, own_sem, send_sem, recv_sem,
 ):
     dom, pencil = lax.axis_index("dom"), lax.axis_index("pencil")
     me = dom * PENCILS + pencil
     load_now = pltpu.make_async_copy(now, m0, load_sem.at[0])
     load_prev = pltpu.make_async_copy(prev, m_old, load_sem.at[1])
-    load_now.start()
-    load_prev.start()
+    small_loads = [
+        pltpu.make_async_copy(ext_in, ext, load_sem.at[2]),
+        pltpu.make_async_copy(strips_in, strips, load_sem.at[3]),
+    ]
+    for load in (*small_loads, load_now, load_prev):
+        load.start()
     barrier = pltpu.get_barrier_semaphore()
 
-    def device_of(step):
-        peer = lax.rem(me + step, EVERYONE)
-        return peer, (lax.div(peer, PENCILS), lax.rem(peer, PENCILS))
+    doms = [lax.rem(dom + d, DOMS) for d in range(DOMS)]
+
+    def devices(shift, own_pencil=False):
+        around = pencil if own_pencil else lax.rem(pencil + shift, PENCILS)
+        return [(d * PENCILS + around, (d, around)) for d in (doms[1:] if own_pencil else doms)]
 
     def greet(first, count):
+        for shift in range(count):
+            for _, device in devices(first + shift):
+                pl.semaphore_signal(barrier, inc=1, device_id=device, device_id_type=MESH)
+
+    def greet_own():
+        for _, device in devices(0, True):
+            pl.semaphore_signal(barrier, inc=1, device_id=device, device_id_type=MESH)
+
+    def send_row(source, target, leg, peer, device):
+        pltpu.make_async_remote_copy(
+            src_ref=source.at[pl.ds(peer, 1)],
+            dst_ref=target.at[pl.ds(me, 1)],
+            send_sem=send_sem.at[leg],
+            recv_sem=recv_sem.at[leg],
+            device_id=device,
+            device_id_type=MESH,
+        ).start()
+
+    def send_rows(source, target, leg, first, count):
+        for shift in range(count):
+            for peer, device in devices(first + shift):
+                send_row(source, target, leg, peer, device)
+
+    def send_own(source, target, leg):
+        for peer, device in devices(0, True):
+            send_row(source, target, leg, peer, device)
+
+    def send_turn(source, target, leg, first, count):
         for j in range(count):
-            pl.semaphore_signal(barrier, inc=1, device_id=device_of(first + j)[1], device_id_type=MESH)
-
-    def send_rows(source, target, leg, first, count):
-        for j in range(count):
-            peer, device = device_of(first + j)
+            peer = lax.rem(pencil + first + j, PENCILS)
             pltpu.make_async_remote_copy(
-                src_ref=source.at[pl.ds(peer, 1)],
-                dst_ref=target.at[pl.ds(me, 1)],
+                src_ref=source(peer),
+                dst_ref=target(pencil),
                 send_sem=send_sem.at[leg],
                 recv_sem=recv_sem.at[leg],
-                device_id=device,
+                device_id=(dom, peer),
                 device_id_type=MESH,
             ).start()
+
+    def turn_of(peer):
+        return turn.at[:, :, lax.div(peer, 2), lax.rem(peer, 2)]
+
+    def pieces_of(peer):
+        return pieces.at[:, :, peer]
+
+    def late_turn_of(peer):
+        return late_turn.at[lax.div(peer, 2), lax.rem(peer, 2)]
+
+    def late_of(peer):
+        return late.at[peer]
 
     def wait_rows(source, target, leg):
         pltpu.make_async_copy(source.at[pl.ds(me, 1)], target.at[pl.ds(me, 1)], own_sem.at[leg]).wait()
@@ -123,11 +171,15 @@
             dst_ref=target.at[pl.ds(0, EVERYONE - 1)],
             send_sem=send_sem.at[leg],
             recv_sem=recv_sem.at[leg],
-            device_id=device_of(1)[1],
+            device_id=(doms[1], pencil),
             device_id_type=MESH,
         ).wait()
 
-    length_x, length_z = ext[dom, 0], ext[dom, 1]
+    greet_own()
+    greet(1, 7)
+    for load in small_loads:
+        load.wait()
+    length_x, length_z = ext[0, dom], ext[1, dom]
 
     lanes = iota((BOX, 128), 1)
     slots = lax.rem(lanes, 8)
@@ -137,7 +189,15 @@
     along_z = waves_z.astype(F32) * HALF_PI / row_of(length_z)
     along_z = along_z * along_z
     live_z = (waves_z < length_z).astype(F32)
-    greet(1, 7)
+    def first_tables(step, carry):
+        at = pl.ds(pl.multiple_of(step * 32, 32), 32)
+        near, far = iota((32, BOX), 0) + step * 32, iota((32, BOX), 1)
+        tz_hi[at, :], tz_lo[at, :] = split(cosines(length_z, near, far))
+        ty_hi[at, :], ty_lo[at, :] = split(cosines(jnp.int32(BOX), far, near))
+        greet(8 + step * 3, 3)
+        return carry
+
+    lax.fori_loop(0, 8, first_tables, 0)
     load_now.wait()
     load_prev.wait()
     block = 32
@@ -160,24 +220,50 @@
             pushed[a, at, :] = live * gain
             twice[a, at, :] = twice_cos
             free[a, at, :] = ahead
+            base = live * (twice_cos * ahead - here)
+            mid_hi[a, at, :], mid_lo[a, at, :] = split(dot3(split(base), (tz_hi[...], tz_lo[...])))
             for u, value in enumerate((here, ahead)):
                 faces = dot3(split(value), (face_hi, face_lo))
                 message = jnp.where(groups == u * ROWS + a, faces, message)
         sent[at, :] = message
-        greet(8 + step * 31, 31)
+        greet(32 + step * 4, 4)
         return carry
 
     lax.fori_loop(0, BOX // block, gather_faces, 0)
+    top = iota((32, 8, BOX), 1) < 4
+
+    def weave(first, second):
+        upper = top[:, :, : first.shape[2]]
+        even = jnp.where(upper, first, pltpu.roll(second, 4, 1))
+        return even, jnp.where(upper, pltpu.roll(first, 4, 1), second)
+
+    for pair in range(2):
+        planes = [
+            dot3((ty_hi[...], ty_lo[...]), (mid_hi[a], mid_lo[a])).reshape(32, 8, BOX)
+            for a in (2 * pair, 2 * pair + 1)
+        ]
+        for parity, woven in enumerate(weave(*planes)):
+            for side in range(2):
+                turn[side, pair, :, parity] = woven[:, :, 128 * side : 128 * side + 128]
     pl.semaphore_wait(barrier, EVERYONE - 1)
     pltpu.make_async_copy(sent.at[pl.ds(me, 1)], got.at[pl.ds(me, 1)], own_sem.at[0]).start()
+    send_own(sent, got, 0)
     send_rows(sent, got, 0, 1, 7)
+    own_turn = pltpu.make_async_copy(turn_of(pencil), pieces_of(pencil), own_sem.at[2])
+    own_turn.start()
+    bulk_one, bulk_two, bulk_three, bulk_four = BULK
+    bulk_after_one = 1 + DOMS * ROWS * bulk_one
+    bulk_after_two = bulk_after_one + DOMS * 2 * bulk_two
+    bulk_after_three = bulk_after_two + bulk_three
+    bulk_after_four = bulk_after_three + 8 * bulk_four
 
     def x_tables(step, carry):
-        send_rows(sent, got, 0, 8 + step * 10, 10)
+        send_rows(sent, got, 0, 8 + step * 3, 3)
+        send_turn(turn_of, pieces_of, 2, 1 + step * bulk_one, bulk_one)
         part, a = lax.div(step, ROWS), lax.rem(step, ROWS)
         at = pl.ds(pl.multiple_of(a * PENCILS, PENCILS), PENCILS)
         high, low = split(
-            cosines(ext[part, 0], iota((PENCILS, BOX), 0) * ROWS + a, iota((PENCILS, BOX), 1))
+            cosines(ext[0, part], iota((PENCILS, BOX), 0) * ROWS + a, iota((PENCILS, BOX), 1))
         )
         tx_hi[part, at, :] = high
         tx_lo[part, at, :] = low
@@ -186,9 +272,10 @@
     lax.fori_loop(0, DOMS * ROWS, x_tables, 0)
 
     def responses(step, carry):
-        send_rows(sent, got, 0, 168 + step * 11, 11)
+        send_rows(sent, got, 0, 56 + step, 1)
+        send_turn(turn_of, pieces_of, 2, bulk_after_one + step * bulk_two, bulk_two)
         part, half = lax.div(step, 2), lax.rem(step, 2)
-        long_x, long_z = ext[part, 0], ext[part, 1]
+        long_x, long_z = ext[0, part], ext[1, part]
         slot = iota((8, BOX), 0)
         rows = jnp.where(slot < 6, cosines(long_z, iota((8, BOX), 1), slot_cells(long_z, slot)), 0.0)
         pairs = jnp.concatenate([rows * rows[i : i + 1] for i in range(8)], axis=0)
@@ -249,6 +336,7 @@
         return [dot_thin(forcing[8 * p : 8 * p + 8], (tx_hi[p], tx_lo[p]), 1) for p in range(DOMS)]
 
     wait_rows(sent, got, 0)
+    send_turn(turn_of, pieces_of, 2, bulk_after_two, bulk_three)
     first, second = [], []
     for pair in range(2):
         turned = got[128 * pair : 128 * pair + 128, :].T
@@ -280,91 +368,113 @@
         rows.append(jnp.zeros((64, 128), F32))
         back[128 * pair : 128 * pair + 128, :] = jnp.concatenate(rows, axis=0).T
     pltpu.make_async_copy(back.at[pl.ds(me, 1)], returned.at[pl.ds(me, 1)], own_sem.at[1]).start()
-    send_rows(back, returned, 1, 1, 15)
+    send_own(back, returned, 1)
+    send_rows(back, returned, 1, 1, 7)
+
+    chunk = iota((1, 128), 1)
+    later, power = lax.div(chunk, 64), lax.rem(lax.div(chunk, 8), 8)
+    rows_of = []
+    for m in range(8):
+        row = jnp.zeros((1, 128), F32)
+        for u, coefs in enumerate((PUSHED_GAIN, GAIN)):
+            for j in range(len(coefs) - m):
+                coef = coefs[m + j] * math.comb(m + j, j) * MID**j
+                row = jnp.where((later == u) & (power == j), coef, row)
+        rows_of.append(row)
 
     def late_tables(step, carry):
-        send_rows(back, returned, 1, 16 + step * 30, 30)
+        send_rows(back, returned, 1, 8 + step * 7, 7)
+        send_turn(turn_of, pieces_of, 2, bulk_after_three + step * bulk_four, bulk_four)
         at = pl.ds(pl.multiple_of(step * 32, 32), 32)
-        near, far = iota((32, BOX), 0) + step * 32, iota((32, BOX), 1)
-        tz_hi[at, :], tz_lo[at, :] = split(cosines(length_z, near, far))
-        ty_hi[at, :], ty_lo[at, :] = split(cosines(jnp.int32(BOX), far, near))
         rows = iota((128, BOX), 0)
         cells = lax.rem(rows, 8)
         values = cosines(length_z, iota((128, BOX), 1), slot_cells(length_z, cells))
         values = jnp.where((cells < 6) & (lax.div(rows, 8) == step), values, 0.0)
         edge_hi[step], edge_lo[step] = split(values)
+        order = iota((32, BOX), 1)
+        waves = lax.rem(order, PENCILS) * ROWS + lax.div(order, PENCILS)
+        xt_hi[at, :], xt_lo[at, :] = split(cosines(length_x, waves, iota((32, BOX), 0) + step * 32))
+        along_y = (iota((32, 128), 0) + step * 32).astype(F32) * (HALF_PI / BOX)
+        along_y = along_y * along_y + MID
+        for a in range(ROWS):
+            wave = pencil * ROWS + a
+            along_x = row_of(wave) * HALF_PI / row_of(length_x)
+            t = along_y + (along_x * along_x)[:, :128]
+            value = rows_of[7] * t + rows_of[6]
+            for m in range(5, -1, -1):
+                value = value * t + rows_of[m]
+            lift[a, at, :] = jnp.where(jnp.full((1, 128), wave) < length_x, value, 0.0)
         return carry
 
     lax.fori_loop(0, 8, late_tables, 0)
+    send_turn(turn_of, pieces_of, 2, bulk_after_four, PENCILS - bulk_after_four)
+    rows = iota((64, BOX), 0)
+    cells = lax.rem(rows, 8)
+    values = jnp.where(cells < 6, cosines(length_z, iota((64, BOX), 1), slot_cells(length_z, cells)), 0.0)
+    offset = along_z * (1.0 / MID) - 1.0
+    raised, factor = jnp.ones_like(values), jnp.broadcast_to(offset, (64, BOX))
+    for j in range(1, 8):
+        raised = jnp.where(lax.div(rows, 8) >= j, raised * factor, raised)
+    spread = dot3(split(values * raised), (tz_hi[...], tz_lo[...]))
+    nothing = jnp.zeros_like(spread)
+    for a in range(2):
+        zt_hi[a], zt_lo[a] = split(jnp.concatenate([nothing, spread] if a else [spread, nothing], axis=0))
+
     wait_rows(back, returned, 1)
     come = split(returned[...])
-    top = iota((32, 8, BOX), 1) < 4
-    own_turns = []
+    source, goal = iota((128, 128), 0), iota((128, 128), 1)
+    half = iota((BOX, 128), 1) < 64
+    planes = []
     for pair in range(2):
-        planes = []
+        lifted = []
         for a in (2 * pair, 2 * pair + 1):
-            wave = pencil * ROWS + a
-            live = live_z * (jnp.full((1, BOX), wave) < length_x).astype(F32)
-            for half in range(2):
-                at = slice(128 * half, 128 * half + 128)
-                left = (come[0][at], come[1][at])
-                gain = pushed[a, at, :]
-                m1 = free[a, at, :] + gain * dot3(left, (edge_hi[a], edge_lo[a]))
-                one_out[a, at, :] = m1
-                m2 = live * (twice[a, at, :] * m1 - m0[a, at, :]) + gain * dot3(
-                    left, (edge_hi[ROWS + a], edge_lo[ROWS + a])
-                )
-                two_out[a, at, :] = m2
-                middle = dot3(split(m2), (tz_hi[...], tz_lo[...]))
-                mid_hi[at, :], mid_lo[at, :] = split(middle)
-            plane = dot3((ty_hi[...], ty_lo[...]), (mid_hi[...], mid_lo[...]))
-            planes.append(plane.reshape(32, 8, BOX))
-        even = jnp.where(top, planes[0], pltpu.roll(planes[1], 4, 1))
-        odd = jnp.where(top, pltpu.roll(planes[0], 4, 1), planes[1])
-        for side in range(2):
-            turn[side, pair, :, 0] = even[:, :, 128 * side : 128 * side + 128]
-            turn[side, pair, :, 1] = odd[:, :, 128 * side : 128 * side + 128]
-        own = pltpu.make_async_copy(
-            turn.at[:, pair, lax.div(pencil, 2), lax.rem(pencil, 2)], pieces.at[:, pair, pencil], own_sem.at[2 + pair]
-        )
-        own.start()
-        own_turns.append(own)
-
-        def send_turn(step, carry):
-            peer = lax.rem(pencil + step, PENCILS)
-            pltpu.make_async_remote_copy(
-                src_ref=turn.at[:, pair, lax.div(peer, 2), lax.rem(peer, 2)],
-                dst_ref=pieces.at[:, pair, pencil],
-                send_sem=send_sem.at[2 + pair],
-                recv_sem=recv_sem.at[2 + pair],
-                device_id=(dom, peer),
-                device_id_type=MESH,
-            ).start()
-            return carry
-
-        lax.fori_loop(1, PENCILS, send_turn, 0)
-
-    def turned_tables(step, carry):
-        at = pl.ds(pl.multiple_of(step * 32, 32), 32)
-        order = iota((32, BOX), 1)
-        waves = lax.rem(lax.div(order, 2), PENCILS) * ROWS + lax.div(order, 128) * 2 + lax.rem(order, 2)
-        xt_hi[at, :], xt_lo[at, :] = split(cosines(length_x, waves, iota((32, BOX), 0) + step * 32))
+            pick = (source == lax.div(goal, 64) * (8 * ROWS) + 8 * a + lax.rem(goal, 8)).astype(F32).astype(BF16)
+            value = (dot(come[0], pick, 1, 0) + dot(come[1], pick, 1, 0)) * lift[a]
+            lifted.append(value + pltpu.roll(value, 64, 1))
+        plane = dot3((ty_hi[...], ty_lo[...]), split(jnp.where(half, lifted[0], lifted[1])))
+        planes.append(plane.reshape(32, 8, 128))
+    for parity, woven in enumerate(weave(*planes)):
+        late_turn[:, parity] = woven
+    own_late = pltpu.make_async_copy(late_turn_of(pencil), late_of(pencil), own_sem.at[3])
+    own_late.start()
+
+    def send_late(step, carry):
+        send_turn(late_turn_of, late_of, 3, 1 + step * 9, 9)
         return carry
 
-    lax.fori_loop(0, 8, turned_tables, 0)
-    for pair in range(2):
-        own_turns[pair].wait()
-        pltpu.make_async_remote_copy(
-            src_ref=pieces.at[:, pair, pl.ds(0, PENCILS - 1)],
-            dst_ref=pieces.at[:, pair, pl.ds(0, PENCILS - 1)],
-            send_sem=send_sem.at[2 + pair],
-            recv_sem=recv_sem.at[2 + pair],
-            device_id=(dom, lax.rem(pencil + 1, PENCILS)),
-            device_id_type=MESH,
-        ).wait()
-
-
-def spread_kernel(pieces, xt_hi, xt_lo, one, two, one_out, two_out, pressure, sems):
+    lax.fori_loop(0, 7, send_late, 0)
+    for a in range(ROWS):
+        live = live_z * (jnp.full((1, BOX), pencil * ROWS + a) < length_x).astype(F32)
+        for piece in range(2):
+            at = slice(128 * piece, 128 * piece + 128)
+            left = (come[0][at], come[1][at])
+            gain = pushed[a, at, :]
+            m1 = free[a, at, :] + gain * dot3(left, (edge_hi[a], edge_lo[a]))
+            one_out[a, at, :] = m1
+            two_out[a, at, :] = live * (twice[a, at, :] * m1 - m0[a, at, :]) + gain * dot3(
+                left, (edge_hi[ROWS + a], edge_lo[ROWS + a])
+            )
+    own_turn.wait()
+    own_late.wait()
+    pltpu.make_async_remote_copy(
+        src_ref=pieces.at[:, :, pl.ds(0, PENCILS - 1)],
+        dst_ref=pieces.at[:, :, pl.ds(0, PENCILS - 1)],
+        send_sem=send_sem.at[2],
+        recv_sem=recv_sem.at[2],
+        device_id=(dom, lax.rem(pencil + 1, PENCILS)),
+        device_id_type=MESH,
+    ).wait()
+    pltpu.make_async_remote_copy(
+        src_ref=late.at[pl.ds(0, PENCILS - 1)],
+        dst_ref=late.at[pl.ds(0, PENCILS - 1)],
+        send_sem=send_sem.at[3],
+        recv_sem=recv_sem.at[3],
+        device_id=(dom, lax.rem(pencil + 1, PENCILS)),
+        device_id_type=MESH,
+    ).wait()
+
+
+def spread_kernel(pieces, late, xt_hi, xt_lo, zt_hi, zt_lo, one, two, one_out, two_out, pressure, sems):
     copies = [
         pltpu.make_async_copy(one, one_out, sems.at[0]),
         pltpu.make_async_copy(two, two_out, sems.at[1]),
@@ -373,45 +483,65 @@
         copy.start()
     table = (xt_hi[...], xt_lo[...])
     for y in range(ROWS):
+        rows = [late[pl.ds(ROWS * pair + y, PENCILS, stride=8), :] for pair in range(2)]
+        rows = split(jnp.concatenate(rows, axis=0))
+        extra = [dot3(rows, (zt_hi[a], zt_lo[a])) for a in range(2)]
         for side in range(2):
-            piece = pieces[pl.ds(side * BOX * ROWS + y, BOX, stride=ROWS), :]
-            pressure[:, y, 128 * side : 128 * side + 128] = dot3(table, split(piece))
+            parts = []
+            for a in range(ROWS):
+                pair, odd = a // 2, a % 2
+                first = side * BOX * ROWS + pair * 8 * PENCILS + odd * ROWS + y
+                piece = pieces[pl.ds(first, PENCILS, stride=8), :]
+                parts.append(piece + extra[odd][PENCILS * pair : PENCILS * (pair + 1), 128 * side : 128 * side + 128])
+            pressure[:, y, 128 * side : 128 * side + 128] = dot3(table, split(jnp.concatenate(parts, axis=0)))
     for copy in copies:
         copy.wait()
 
 
 def on_device(modes_now, modes_prev, extents, strips):
-    vmem, smem, anywhere = (
-        pl.BlockSpec(memory_space=space) for space in (pltpu.VMEM, pltpu.SMEM, pl.ANY)
+    vmem, hbm, anywhere = (
+        pl.BlockSpec(memory_space=space) for space in (pltpu.VMEM, pltpu.HBM, pl.ANY)
     )
     field = jax.ShapeDtypeStruct((ROWS, BOX, BOX), F32)
     half_table = jax.ShapeDtypeStruct((BOX, BOX), BF16)
-    one, two, pieces, xt_hi, xt_lo = pl.pallas_call(
+    wide_table = jax.ShapeDtypeStruct((2, 128, BOX), BF16)
+    one, two, pieces, late, xt_hi, xt_lo, zt_hi, zt_lo = pl.pallas_call(
         coupled_kernel,
-        out_shape=(field, field, jax.ShapeDtypeStruct((2, 2, PENCILS, 8, 128), F32), half_table, half_table),
-        in_specs=[smem, smem, anywhere, anywhere],
-        out_specs=[vmem] * 5,
+        out_shape=(
+            field,
+            field,
+            jax.ShapeDtypeStruct((2, 2, PENCILS, 8, 128), F32),
+            jax.ShapeDtypeStruct((PENCILS, 8, 128), F32),
+            half_table,
+            half_table,
+            wide_table,
+            wide_table,
+        ),
+        in_specs=[hbm] * 4,
+        out_specs=[vmem] * 8,
         scratch_shapes=[pltpu.VMEM((ROWS, BOX, BOX), F32)] * 5
         + [pltpu.VMEM((EVERYONE, 128), F32)] * 4
         + [pltpu.VMEM((DOMS, BOX, BOX), BF16)] * 2
         + [pltpu.VMEM((DOMS, 2, 64, 128), F32)]
         + [pltpu.VMEM((2 * ROWS, 128, BOX), BF16)] * 2
-        + [pltpu.VMEM((BOX, BOX), BF16)] * 6
+        + [pltpu.VMEM((BOX, BOX), BF16)] * 4
+        + [pltpu.VMEM((ROWS, BOX, BOX), BF16)] * 2
         + [pltpu.VMEM((2, 2, PENCILS // 2, 2, 8, 128), F32)]
-        + [pltpu.SemaphoreType.DMA((2,))]
-        + [pltpu.SemaphoreType.DMA((4,))] * 3,
-        compiler_params=pltpu.CompilerParams(has_side_effects=True, collective_id=1, vmem_limit_bytes=44 << 20),
+        + [pltpu.VMEM((ROWS, BOX, 128), F32), pltpu.VMEM((PENCILS // 2, 2, 8, 128), F32)]
+        + [pltpu.SMEM((2, DOMS), I32), pltpu.SMEM((STRIPS, 6), I32)]
+        + [pltpu.SemaphoreType.DMA((4,))] * 4,
+        compiler_params=pltpu.CompilerParams(has_side_effects=True, collective_id=1, vmem_limit_bytes=199 << 18),
         name="coupled",
-    )(extents, strips, modes_now[0], modes_prev[0])
+    )(extents.T, strips, modes_now[0], modes_prev[0])
     one, two, pressure = pl.pallas_call(
         spread_kernel,
         out_shape=(field, field, jax.ShapeDtypeStruct((BOX, ROWS, BOX), F32)),
-        in_specs=[vmem] * 5,
+        in_specs=[vmem] * 8,
         out_specs=[anywhere, anywhere, vmem],
         scratch_shapes=[pltpu.SemaphoreType.DMA((2,))],
         compiler_params=pltpu.CompilerParams(vmem_limit_bytes=24 << 20),
         name="spread",
-    )(pieces.reshape(2 * BOX * ROWS, 128), xt_hi, xt_lo, one, two)
+    )(pieces.reshape(2 * BOX * ROWS, 128), late.reshape(PENCILS * 8, 128), xt_hi, xt_lo, zt_hi, zt_lo, one, two)
     return (two[None], one[None], pressure[None])
 
 

time: 71 us -> 64.8 us (0.913)
  Pallas kernels: 67 us -> 63.3 us
  local copies, waits for them, and re-layouts: 3.22 us -> 0.68 us
    pallas_call x1, Pallas kernels: 64.6 us -> 59.8 us  [on_device(): pl.pallas_call(coupled_kernel, out_shape=(field, field, jax.ShapeDtypeStr...]
    unnamed x7 -> x4, local copies, waits for them, and re-layouts: 3.22 us -> 0.68 us
    pallas_call x1, Pallas kernels: 2.36 us -> 3.47 us  [on_device(): pl.pallas_call(spread_kernel, out_shape=(field, field, jax.ShapeDtypeStru...]
where the time goes in v1:
time: 64.8 us; the launch traced here: 64.6 us
  Pallas kernels  63.3 us (98%)
  local copies, waits for them, and re-layouts  0.68 us (1%)
  between operations  0.66 us (1%)
    pallas_call x1, Pallas kernels, on_device(): pl.pallas_call(coupled_kernel, out_shape=(field, field, jax.ShapeDtypeStr...  59.8 us
    pallas_call x1, Pallas kernels, on_device(): pl.pallas_call(spread_kernel, out_shape=(field, field, jax.ShapeDtypeStru...  3.47 us

profile of v1, /device:TPU:1, one launch (start us, length us, event | category | flops | bytes accessed | tf_op | source)
XLA Modules:
  0.0 64.6 jit_solution(8693843111315343768)
XLA Ops:
  0.6 0.0 copy-start
  0.6 0.0 copy-start.1
  0.7 0.7 %copy-done = s32[8,6]{1,0:T(8,128)S(1)} copy-done((s32[8,6]{1,0:T(8,128)S(1)}, s32[8,6]{1,0:T(8,128)}, u32[]{:S(2)}) %copy-start) | copy-done | bytes 216
  1.3 0.0 copy-done.1
  1.3 59.8 %coupled.1 = (f32[4,256,256]{2,1,0:T(8,128)S(1)}, f32[4,256,256]{2,1,0:T(8,128)S(1)}, f32[2,2,64,8,128]{4,3,2,1,0:T(8,128)S(1)}, f32[64,8,128]{2,1,0:T(8,128)S(1...) custom-call(s32[2,4]{1,0:T(2,128)S(1)} %bitcast.10, ...), custom_call_target="tpu_custom_call" | custom-call | tf_op jit(solution)/shard_map/coupled/pallas_call | solution.py:508
  61.2 3.5 %spread.1 = (f32[4,256,256]{2,1,0:T(8,128)}, f32[4,256,256]{2,1,0:T(8,128)}, f32[256,4,256]{2,1,0:T(4,128)}) custom-call(f32[2048,128]{1,0:T(8,128)S(1)} %bitcast.8, f32[512,128]{1,0:T(8,128)S(1)} %bitcast.9, bf16[256,256]{1,0:T(8,128)(2,1)S(1)} %get-tuple-element.16.xt_hi, bf16[256,256]{1,0:T(8,128)(2,1)S(1)} %get-tuple-element.17.xt_lo, ...), custom_call_target="tpu_custom_call" | custom-call | tf_op jit(solution)/shard_map/spread/pallas_call | solution.py:536
Async XLA Ops:
  0.6 0.7 %copy-start = (s32[8,6]{1,0:T(8,128)S(1)}, s32[8,6]{1,0:T(8,128)}, u32[]{:S(2)}) copy-start(s32[8,6]{1,0:T(8,128)} %strips_in.1) | copy-start | bytes 580
  0.6 0.7 %copy-start.1 = (s32[4,2]{0,1:T(2,128)S(1)}, s32[4,2]{0,1:T(2,128)}, u32[]{:S(2)}) copy-start(s32[4,2]{0,1:T(2,128)} %param.6) | copy-start | bytes 100

commit v2 on v1

--- a/solution.py
+++ b/solution.py
@@ -24,7 +24,8 @@
     0.0005628010719150018, -1.6955597515164814e-05, 3.5301674212625207e-07, -4.241805096348839e-09,
 )
 MID = math.pi**2 / 8.0
-BULK = (1, 2, 16, 0)
+PARTS = 2
+BULK = (1,2,12,0)
 SINE = (
     1.5707963267681446, -0.6459640955780578, 0.07969260371703452, -0.004681657795344663,
     0.00016025469086571314, -3.431829236433259e-06,
@@ -474,26 +475,35 @@
     ).wait()
 
 
-def spread_kernel(pieces, late, xt_hi, xt_lo, zt_hi, zt_lo, one, two, one_out, two_out, pressure, sems):
+def spread_kernel(pieces, late, xt_hi, xt_lo, zt_hi, zt_lo, one, two, one_out, two_out, pressure, held, sems):
     copies = [
         pltpu.make_async_copy(one, one_out, sems.at[0]),
         pltpu.make_async_copy(two, two_out, sems.at[1]),
     ]
     for copy in copies:
         copy.start()
-    table = (xt_hi[...], xt_lo[...])
+    fields = []
     for y in range(ROWS):
         rows = [late[pl.ds(ROWS * pair + y, PENCILS, stride=8), :] for pair in range(2)]
         rows = split(jnp.concatenate(rows, axis=0))
         extra = [dot3(rows, (zt_hi[a], zt_lo[a])) for a in range(2)]
-        for side in range(2):
-            parts = []
-            for a in range(ROWS):
-                pair, odd = a // 2, a % 2
-                first = side * BOX * ROWS + pair * 8 * PENCILS + odd * ROWS + y
-                piece = pieces[pl.ds(first, PENCILS, stride=8), :]
-                parts.append(piece + extra[odd][PENCILS * pair : PENCILS * (pair + 1), 128 * side : 128 * side + 128])
-            pressure[:, y, 128 * side : 128 * side + 128] = dot3(table, split(jnp.concatenate(parts, axis=0)))
+        parts = []
+        for a in range(ROWS):
+            pair, odd = a // 2, a % 2
+            sides = [
+                pieces[pl.ds(side * BOX * ROWS + pair * 8 * PENCILS + odd * ROWS + y, PENCILS, stride=8), :]
+                for side in range(2)
+            ]
+            parts.append(jnp.concatenate(sides, axis=1) + extra[odd][PENCILS * pair : PENCILS * (pair + 1)])
+        fields.append(split(jnp.concatenate(parts, axis=0)))
+    for part in range(PARTS):
+        at = slice(part * (BOX // PARTS), (part + 1) * (BOX // PARTS))
+        table = (xt_hi[at, :], xt_lo[at, :])
+        for y in range(ROWS):
+            held[at, y, :] = dot3(table, fields[y])
+        copy = pltpu.make_async_copy(held.at[at], pressure.at[at], sems.at[2 + part])
+        copy.start()
+        copies.append(copy)
     for copy in copies:
         copy.wait()
 
@@ -537,8 +547,8 @@
         spread_kernel,
         out_shape=(field, field, jax.ShapeDtypeStruct((BOX, ROWS, BOX), F32)),
         in_specs=[vmem] * 8,
-        out_specs=[anywhere, anywhere, vmem],
-        scratch_shapes=[pltpu.SemaphoreType.DMA((2,))],
+        out_specs=[anywhere] * 3,
+        scratch_shapes=[pltpu.VMEM((BOX, ROWS, BOX), F32), pltpu.SemaphoreType.DMA((2 + PARTS,))],
         compiler_params=pltpu.CompilerParams(vmem_limit_bytes=24 << 20),
         name="spread",
     )(pieces.reshape(2 * BOX * ROWS, 128), late.reshape(PENCILS * 8, 128), xt_hi, xt_lo, zt_hi, zt_lo, one, two)

time: 64.8 us -> 63.1 us (0.974)
  Pallas kernels: 63.3 us -> 61.7 us
    pallas_call x1, Pallas kernels: 3.47 us -> 2.35 us  [on_device(): pl.pallas_call(spread_kernel, out_shape=(field, field, jax.ShapeDtypeStru...]
where the time goes in v2:
time: 63.1 us; the launch traced here: 63 us
  Pallas kernels  61.7 us (98%)
  local copies, waits for them, and re-layouts  0.68 us (1%)
  between operations  0.66 us (1%)
    pallas_call x1, Pallas kernels, on_device(): pl.pallas_call(coupled_kernel, out_shape=(field, field, jax.ShapeDtypeStr...  59.3 us
    pallas_call x1, Pallas kernels, on_device(): pl.pallas_call(spread_kernel, out_shape=(field, field, jax.ShapeDtypeStru...  2.35 us

profile of v2, /device:TPU:1, one launch (start us, length us, event | category | flops | bytes accessed | tf_op | source)
XLA Modules:
  0.0 63.0 jit_solution(3223741599968209128)
XLA Ops:
  0.6 0.0 copy-start
  0.6 0.0 copy-start.1
  0.7 0.7 %copy-done = s32[8,6]{1,0:T(8,128)S(1)} copy-done((s32[8,6]{1,0:T(8,128)S(1)}, s32[8,6]{1,0:T(8,128)}, u32[]{:S(2)}) %copy-start) | copy-done | bytes 216
  1.3 0.0 copy-done.1
  1.3 59.3 %coupled.1 = (f32[4,256,256]{2,1,0:T(8,128)S(1)}, f32[4,256,256]{2,1,0:T(8,128)S(1)}, f32[2,2,64,8,128]{4,3,2,1,0:T(8,128)S(1)}, f32[64,8,128]{2,1,0:T(8,128)S(1...) custom-call(s32[2,4]{1,0:T(2,128)S(1)} %bitcast.10, ...), custom_call_target="tpu_custom_call" | custom-call | tf_op jit(solution)/shard_map/coupled/pallas_call | solution.py:518
  60.7 2.4 %spread.1 = (f32[4,256,256]{2,1,0:T(8,128)}, f32[4,256,256]{2,1,0:T(8,128)}, f32[256,4,256]{2,1,0:T(4,128)}) custom-call(f32[2048,128]{1,0:T(8,128)S(1)} %bitcast.8, f32[512,128]{1,0:T(8,128)S(1)} %bitcast.9, bf16[256,256]{1,0:T(8,128)(2,1)S(1)} %get-tuple-element.16.xt_hi, bf16[256,256]{1,0:T(8,128)(2,1)S(1)} %get-tuple-element.17.xt_lo, ...), custom_call_target="tpu_custom_call" | custom-call | tf_op jit(solution)/shard_map/spread/pallas_call | solution.py:546
Async XLA Ops:
  0.6 0.7 %copy-start = (s32[8,6]{1,0:T(8,128)S(1)}, s32[8,6]{1,0:T(8,128)}, u32[]{:S(2)}) copy-start(s32[8,6]{1,0:T(8,128)} %strips_in.1) | copy-start | bytes 580
  0.6 0.7 %copy-start.1 = (s32[4,2]{0,1:T(2,128)S(1)}, s32[4,2]{0,1:T(2,128)}, u32[]{:S(2)}) copy-start(s32[4,2]{0,1:T(2,128)} %param.6) | copy-start | bytes 100

commit v3 on v2

--- a/solution.py
+++ b/solution.py
@@ -336,8 +336,8 @@
         forcing = dot(gives, gap[0], 1, 0) + dot(gives, gap[1], 1, 0)
         return [dot_thin(forcing[8 * p : 8 * p + 8], (tx_hi[p], tx_lo[p]), 1) for p in range(DOMS)]
 
+    send_turn(turn_of, pieces_of, 2, bulk_after_two, bulk_three)
     wait_rows(sent, got, 0)
-    send_turn(turn_of, pieces_of, 2, bulk_after_two, bulk_three)
     first, second = [], []
     for pair in range(2):
         turned = got[128 * pair : 128 * pair + 128, :].T

time: 63.1 us -> 60.2 us (0.954)
  Pallas kernels: 61.7 us -> 58.8 us
    pallas_call x1, Pallas kernels: 59.3 us -> 56.4 us  [on_device(): pl.pallas_call(coupled_kernel, out_shape=(field, field, jax.ShapeDtypeStr...]
where the time goes in v3:
time: 60.2 us; the launch traced here: 60.1 us
  Pallas kernels  58.8 us (98%)
  local copies, waits for them, and re-layouts  0.68 us (1%)
  between operations  0.66 us (1%)
    pallas_call x1, Pallas kernels, on_device(): pl.pallas_call(coupled_kernel, out_shape=(field, field, jax.ShapeDtypeStr...  56.4 us
    pallas_call x1, Pallas kernels, on_device(): pl.pallas_call(spread_kernel, out_shape=(field, field, jax.ShapeDtypeStru...  2.35 us

profile of v3, /device:TPU:1, one launch (start us, length us, event | category | flops | bytes accessed | tf_op | source)
XLA Modules:
  0.0 60.1 jit_solution(6883569480438672064)
XLA Ops:
  0.6 0.0 copy-start
  0.6 0.0 copy-start.1
  0.7 0.7 %copy-done = s32[8,6]{1,0:T(8,128)S(1)} copy-done((s32[8,6]{1,0:T(8,128)S(1)}, s32[8,6]{1,0:T(8,128)}, u32[]{:S(2)}) %copy-start) | copy-done | bytes 216
  1.3 0.0 copy-done.1
  1.3 56.4 %coupled.1 = (f32[4,256,256]{2,1,0:T(8,128)S(1)}, f32[4,256,256]{2,1,0:T(8,128)S(1)}, f32[2,2,64,8,128]{4,3,2,1,0:T(8,128)S(1)}, f32[64,8,128]{2,1,0:T(8,128)S(1...) custom-call(s32[2,4]{1,0:T(2,128)S(1)} %bitcast.10, ...), custom_call_target="tpu_custom_call" | custom-call | tf_op jit(solution)/shard_map/coupled/pallas_call | solution.py:518
  57.8 2.3 %spread.1 = (f32[4,256,256]{2,1,0:T(8,128)}, f32[4,256,256]{2,1,0:T(8,128)}, f32[256,4,256]{2,1,0:T(4,128)}) custom-call(f32[2048,128]{1,0:T(8,128)S(1)} %bitcast.8, f32[512,128]{1,0:T(8,128)S(1)} %bitcast.9, bf16[256,256]{1,0:T(8,128)(2,1)S(1)} %get-tuple-element.16.xt_hi, bf16[256,256]{1,0:T(8,128)(2,1)S(1)} %get-tuple-element.17.xt_lo, ...), custom_call_target="tpu_custom_call" | custom-call | tf_op jit(solution)/shard_map/spread/pallas_call | solution.py:546
Async XLA Ops:
  0.6 0.7 %copy-start = (s32[8,6]{1,0:T(8,128)S(1)}, s32[8,6]{1,0:T(8,128)}, u32[]{:S(2)}) copy-start(s32[8,6]{1,0:T(8,128)} %strips_in.1) | copy-start | bytes 580
  0.6 0.7 %copy-start.1 = (s32[4,2]{0,1:T(2,128)S(1)}, s32[4,2]{0,1:T(2,128)}, u32[]{:S(2)}) copy-start(s32[4,2]{0,1:T(2,128)} %param.6) | copy-start | bytes 100
